TPU v7x, 128 devices: a whole 4x4x4 slice. The times are simulated.
128 devices in a mesh: dp: 8 (over y, core), expert: 16 (over x, z).
Axes of the slice: x: 4, y: 4, z: 4, core: 2. Of those that a mesh axis runs over, the one named last changes fastest.
Arguments:
- tokens: bfloat16 [2048, 3072], P('expert', 'dp'), may hold values from -6 to 6
- grad_out: bfloat16 [2048, 3072], P('expert', 'dp'), may hold values from -0.59765625 to 0.59765625
- routes: int32 [2048, 4], P('expert'), may hold values from 0 to 15, all different within a row; in each aligned block of 128 rows (0 to 127, 128 to 255, ...) at most 48 rows name the same one
- gate_values: bfloat16 [2048, 4], P('expert'), may hold values from 0.099609375 to 1
- w_gate: bfloat16 [16, 5376, 3072], P('expert', 'dp'), may hold values from -0.109375 to 0.109375
- w_up: bfloat16 [16, 5376, 3072], P('expert', 'dp'), may hold values from -0.109375 to 0.109375
- w_down: bfloat16 [16, 5376, 3072], P('expert', 'dp'), may hold values from -0.078125 to 0.078125
Outputs:
- grad_tokens: bfloat16 [2048, 3072], P('expert', 'dp')
- grad_gates: float32 [2048, 4], P('expert')
- grad_w_gate: bfloat16 [16, 5376, 3072], P('expert', 'dp')
- grad_w_up: bfloat16 [16, 5376, 3072], P('expert', 'dp')
- grad_w_down: bfloat16 [16, 5376, 3072], P('expert', 'dp')
Inputs may be any that keep to these rules, and one draw needn't show every extreme that they name: `routes`: the 4 experts of a token differ. Among the 128 tokens of one index of the expert axis (aligned blocks of tokens) no expert is chosen more than 48 times, and in every draw some expert is chosen exactly 48 times in some block.
All inputs are finite; a program needn't handle non-finite values.
Results may differ from a plain program's by a relative error of at most 0.011.
Values may be sent and summed in bfloat16 or wider, within the bound.
A program may use at most 128 MiB of HBM per device.

v0:
```python
import jax
import jax.numpy as jnp
from jax import lax
from jax.sharding import PartitionSpec as P


def slot_index(block_routes, experts, capacity):
    flattened = block_routes.reshape(-1)
    onehot = (flattened[:, None] == jnp.arange(experts, dtype=jnp.int32)[None, :]).astype(jnp.int32)
    before = jnp.cumsum(onehot, axis=0) - onehot
    position = jnp.sum(before * onehot, axis=1)
    return flattened * capacity + position


def expert_backward(x_rows, dy_rows, gate_rows, weight_gate, weight_up, weight_down):
    pre_gate = jnp.einsum("sd,fd->sf", x_rows, weight_gate, preferred_element_type=jnp.float32)
    pre_up = jnp.einsum("sd,fd->sf", x_rows, weight_up, preferred_element_type=jnp.float32)
    projected = jnp.einsum("sd,fd->sf", dy_rows, weight_down, preferred_element_type=jnp.float32)
    squash = jax.nn.sigmoid(pre_gate)
    activated = pre_gate * squash
    hidden = (activated * pre_up).astype(jnp.bfloat16)
    gate_part = jnp.sum(projected * hidden.astype(jnp.float32), axis=1)
    scale = gate_rows.astype(jnp.float32)[:, None]
    hidden_grad = scale * projected
    d_gate = (hidden_grad * pre_up * squash * (1.0 + pre_gate * (1.0 - squash))).astype(
        jnp.bfloat16
    )
    d_up = (hidden_grad * activated).astype(jnp.bfloat16)
    d_out = (scale * dy_rows.astype(jnp.float32)).astype(jnp.bfloat16)
    input_part = jnp.dot(d_gate, weight_gate, preferred_element_type=jnp.float32) + jnp.dot(
        d_up, weight_up, preferred_element_type=jnp.float32
    )
    grad_gate_w = jnp.einsum(
        "sf,sd->fd", d_gate, x_rows, preferred_element_type=jnp.float32
    ).astype(jnp.bfloat16)
    grad_up_w = jnp.einsum("sf,sd->fd", d_up, x_rows, preferred_element_type=jnp.float32).astype(
        jnp.bfloat16
    )
    grad_down_w = jnp.einsum("sf,sd->fd", hidden, d_out, preferred_element_type=jnp.float32).astype(
        jnp.bfloat16
    )
    return (input_part, gate_part, grad_gate_w, grad_up_w, grad_down_w)


def pack_rows(chooser_half, source, experts, capacity):
    packed = jnp.einsum("ts,td->sd", chooser_half, source, preferred_element_type=jnp.float32)
    return packed.astype(jnp.bfloat16).reshape(experts, capacity, source.shape[1])


def combine_rows(slot_rows, indices, tok_rows, top_count):
    picked = slot_rows[indices]
    return jnp.sum(picked.reshape(tok_rows, top_count, slot_rows.shape[1]), axis=1)


def per_device(tokens, grad_out, routes, gate_values, w_gate, w_up, w_down):
    tok_rows, top_count = routes.shape
    experts = lax.axis_size("expert")
    capacity = tok_rows * top_count * 3 // (2 * experts)
    slot_total = experts * capacity
    indices = slot_index(routes, experts, capacity)
    placed = (indices[:, None] == jnp.arange(slot_total, dtype=jnp.int32)[None, :]).astype(
        jnp.float32
    )
    placed = placed.reshape(tok_rows, top_count, slot_total)
    chooser = jnp.sum(placed, axis=1)
    chooser_half = chooser.astype(jnp.bfloat16)
    slot_gates = jnp.einsum(
        "tks,tk->s", placed, gate_values.astype(jnp.float32), precision=lax.Precision.HIGHEST
    )
    slot_gates = slot_gates.astype(jnp.bfloat16).reshape(experts, capacity)
    full_x, full_dy = (
        lax.all_gather(tokens, "dp", axis=1, tiled=True),
        lax.all_gather(grad_out, "dp", axis=1, tiled=True),
    )
    send_x = pack_rows(chooser_half, full_x, experts, capacity)
    send_dy = pack_rows(chooser_half, full_dy, experts, capacity)
    rows_x, rows_dy, rows_gate = (
        lax.all_to_all(send_x, "expert", split_axis=0, concat_axis=0, tiled=True),
        lax.all_to_all(send_dy, "expert", split_axis=0, concat_axis=0, tiled=True),
        lax.all_to_all(slot_gates, "expert", split_axis=0, concat_axis=0, tiled=True),
    )
    width = rows_x.shape[2]
    input_part, gate_part, grad_gate_w, grad_up_w, grad_down_w = expert_backward(
        rows_x.reshape(slot_total, width),
        rows_dy.reshape(slot_total, width),
        rows_gate.reshape(slot_total),
        w_gate[0],
        w_up[0],
        w_down[0],
    )
    back_grad, back_gate = (
        lax.all_to_all(
            input_part.reshape(experts, capacity, width).astype(jnp.bfloat16),
            "expert",
            split_axis=0,
            concat_axis=0,
            tiled=True,
        ).astype(jnp.float32),
        lax.all_to_all(
            gate_part.reshape(experts, capacity).astype(jnp.bfloat16),
            "expert",
            split_axis=0,
            concat_axis=0,
            tiled=True,
        ).astype(jnp.float32),
    )
    token_grad = combine_rows(back_grad.reshape(slot_total, width), indices, tok_rows, top_count)
    grad_tokens = lax.psum_scatter(token_grad, "dp", scatter_dimension=1, tiled=True).astype(
        jnp.bfloat16
    )
    token_gate = back_gate.reshape(slot_total)[indices].reshape(tok_rows, top_count)
    grad_gates = lax.psum(token_gate, "dp")
    return (grad_tokens, grad_gates, grad_gate_w[None], grad_up_w[None], grad_down_w[None])


def solution(mesh):
    return jax.shard_map(
        per_device,
        mesh=mesh,
        in_specs=(
            P("expert", "dp"),
            P("expert", "dp"),
            P("expert", None),
            P("expert", None),
            P("expert", "dp", None),
            P("expert", "dp", None),
            P("expert", "dp", None),
        ),
        out_specs=(
            P("expert", "dp"),
            P("expert", None),
            P("expert", "dp", None),
            P("expert", "dp", None),
            P("expert", "dp", None),
        ),
        check_vma=False,
    )
```

profile of v0, /device:TPU:2, one launch (start us, length us, event | category | flops | bytes accessed | tf_op | source)
XLA Modules:
  0.0 375.2 jit_solution(11851888171765762990)
XLA Ops:
  11.1 8.3 %all-to-all-start = ((bf16[16,1,48]{2,1,0:T(2,128)(2,1)}), bf16[16,1,48]{2,1,0:T(2,128)(2,1)S(1)}, u32[]{:S(2)}, u32[]{:S(2)}) async-start(bf16[16,1,48]{2,1,0:T(2,128)(2,1)} %all_to_all.25), calls=%async_computation | async-start | bytes 16384 | tf_op jit(solution)/shard_map/all_to_all | solution.py:80
  19.6 14.3 %all_gather.7 = bf16[128,3072]{1,0:T(8,128)(2,1)S(1)} all-gather(bf16[128,384]{1,0:T(8,128)(2,1)} %param.7), channel_id=1, replica_groups=mesh['dp'=8,'expert'=16] {'dp'}, dimensions={1}, use_global_device_ids=true | all-gather | bytes 884736 | tf_op jit(solution)/shard_map/all_gather | solution.py:72
  37.5 7.4 %all-to-all-start.2 = ((bf16[16,48,3072]{2,1,0:T(8,128)(2,1)}), bf16[16,48,3072]{2,1,0:T(8,128)(2,1)}, u32[]{:S(2)}, u32[]{:S(2)}) async-start(bf16[16,48,3072]{2,1,0:T(8,128)(2,1)} %bitcast.67), calls=%async_computation.2 | async-start | bytes 9437184 | tf_op jit(solution)/shard_map/all_to_all | solution.py:78
  44.8 13.6 %all_gather.6 = bf16[128,3072]{1,0:T(8,128)(2,1)S(1)} all-gather(bf16[128,384]{1,0:T(8,128)(2,1)S(1)} %copy-done.3), channel_id=1, replica_groups=mesh['dp'=8,'expert'=16] {'dp'}, dimensions={1}, use_global_device_ids=true | all-gather | bytes 884736 | tf_op jit(solution)/shard_map/all_gather | solution.py:73
  58.4 3.6 convolution_convert_fusion.1
  62.0 44.2 %all-to-all-done.2 = bf16[16,48,3072]{2,1,0:T(8,128)(2,1)} async-done(((bf16[16,48,3072]{2,1,0:T(8,128)(2,1)}), bf16[16,48,3072]{2,1,0:T(8,128)(2,1)}, u32[]{:S(2)}, u32[]{:S(2)}) %all-to-all-start.2) | async-done | bytes 4718624 | tf_op jit(solution)/shard_map/all_to_all | solution.py:78
  106.2 18.2 %all-to-all-start.1 = ((bf16[16,48,3072]{2,1,0:T(8,128)(2,1)}), bf16[16,48,3072]{2,1,0:T(8,128)(2,1)}, u32[]{:S(2)}, u32[]{:S(2)}) async-start(bf16[16,48,3072]{2,1,0:T(8,128)(2,1)} %bitcast.66), calls=%async_computation.1 | async-start | bytes 9437184 | tf_op jit(solution)/shard_map/all_to_all | solution.py:79
  124.5 8.4 %fusion.6 = f32[768,672]{0,1:T(8,128)} fusion(bf16[768,3072]{1,0:T(8,128)(2,1)} %bitcast.6, bf16[1,672,3072]{2,1,0:T(8,128)(2,1)} %param.11), kind=kOutput, calls=%fused_computation.16 | convolution fusion | flops 3170893824 | bytes 10911744 | tf_op jit(solution)/shard_map/sd,fd->sf/dot_general | solution.py:16
  132.9 7.1 %fusion.9 = f32[768,672]{0,1:T(8,128)} fusion(bf16[768,3072]{1,0:T(8,128)(2,1)} %bitcast.6, bf16[1,672,3072]{2,1,0:T(8,128)(2,1)S(1)} %copy-done.4), kind=kOutput, calls=%fused_computation.19 | convolution fusion | flops 3170893824 | bytes 10911744 | tf_op jit(solution)/shard_map/sd,fd->sf/dot_general | solution.py:17
  140.0 43.8 %all-to-all-done.1 = bf16[16,48,3072]{2,1,0:T(8,128)(2,1)} async-done(((bf16[16,48,3072]{2,1,0:T(8,128)(2,1)}), bf16[16,48,3072]{2,1,0:T(8,128)(2,1)}, u32[]{:S(2)}, u32[]{:S(2)}) %all-to-all-start.1) | async-done | bytes 4718624 | tf_op jit(solution)/shard_map/all_to_all | solution.py:79
  183.9 9.1 %multiply_reduce_fusion = (bf16[768]{0:T(1024)(128)(2,1)S(1)}, bf16[768,672]{0,1:T(8,128)(2,1)S(1)}, bf16[768,672]{0,1:T(8,128)(2,1)S(1)}, bf16[768,672]{0,1:T(8,128)(2,1)S(1)}) fusion(f32[768,672]{0,1:T(8,128)} %fusion.9, f32[768,672]{0,1:T(8,128)} %fusion.6, f32[768]{0:T(1024)S(1)} %reshape.144, bf16[768,3072]{1,0:T(8,128)(2,1)} %bitcast.3, ...), kind=kOutput, calls=%fused_computation.23 | convolution fusion | flops 3180698880 | bytes 16077312 | tf_op jit(solution)/shard_map/sd,fd->sf/dot_general | solution.py:18
  193.0 4.2 %fusion.4 = f32[768,3072]{1,0:T(8,128)S(1)} fusion(bf16[768,672]{0,1:T(8,128)(2,1)S(1)} %get-tuple-element.22, bf16[1,672,3072]{2,1,0:T(8,128)(2,1)S(1)} %copy-done.2), kind=kOutput, calls=%fused_computation.14 | convolution fusion | flops 3170893824 | bytes 14598144 | tf_op jit(solution)/shard_map/dot_general | solution.py:30
  197.2 5.9 %add_convert_fusion = bf16[768,3072]{1,0:T(8,128)(2,1)} fusion(f32[768,3072]{1,0:T(8,128)S(1)} %fusion.4, bf16[768,672]{0,1:T(8,128)(2,1)S(1)} %get-tuple-element.23, bf16[1,672,3072]{2,1,0:T(8,128)(2,1)S(1)} %copy-done.5), kind=kOutput, calls=%fused_computation.3 | convolution fusion | flops 3175612416 | bytes 19316736 | tf_op jit(solution)/shard_map/dot_general | solution.py:30
  203.1 16.9 %all-to-all-start.3 = ((bf16[16,48,3072]{2,1,0:T(8,128)(2,1)}), bf16[16,48,3072]{2,1,0:T(8,128)(2,1)}, u32[]{:S(2)}, u32[]{:S(2)}) async-start(bf16[16,48,3072]{2,1,0:T(8,128)(2,1)} %bitcast.68), calls=%async_computation.3 | async-start | bytes 9437184 | tf_op jit(solution)/shard_map/all_to_all | solution.py:92
  220.2 54.7 %all-to-all-done.3 = bf16[16,48,3072]{2,1,0:T(8,128)(2,1)} async-done(((bf16[16,48,3072]{2,1,0:T(8,128)(2,1)}), bf16[16,48,3072]{2,1,0:T(8,128)(2,1)}, u32[]{:S(2)}, u32[]{:S(2)}) %all-to-all-start.3) | async-done | bytes 4718624 | tf_op jit(solution)/shard_map/all_to_all | solution.py:92
  274.9 7.3 %bitcast_convert_fusion = f32[768,3072]{1,0:T(8,128)} fusion(bf16[16,48,3072]{2,1,0:T(8,128)(2,1)} %all-to-all-done.3), kind=kLoop, calls=%fused_computation.9 | loop fusion | flops 2359296 | bytes 14155776 | tf_op jit(solution)/shard_map/reshape | solution.py:107
  282.2 11.0 %gather_fusion = f32[512,3072]{1,0:T(8,128)} fusion(f32[768,3072]{1,0:T(8,128)} %bitcast_convert_fusion, s32[1024]{0:T(1024)S(1)} %pad_clamp_fusion), kind=kCustom, calls=%fused_computation | custom fusion | bytes 12584960 | tf_op jit(solution)/shard_map/gather | solution.py:51
  293.1 7.6 %reshape.142 = f32[128,4,3072]{2,1,0:T(4,128)} reshape(f32[512,3072]{1,0:T(8,128)} %gather_fusion) | data formatting | bytes 12582912 | tf_op jit(solution)/shard_map/reshape | solution.py:52
  300.7 7.7 %reduce_sum.44 = f32[128,3072]{1,0:T(8,128)} reduce(f32[128,4,3072]{2,1,0:T(4,128)} %reshape.142, f32[]{:T(128)} %constant.3.clone.1), dimensions={1}, to_apply=%region_4.5 | reduce | flops 1179648 | bytes 7864324 | tf_op jit(solution)/shard_map/reduce_sum | solution.py:52
  309.1 8.3 %all-to-all-start.4 = ((bf16[16,1,48]{2,1,0:T(2,128)(2,1)}), bf16[16,1,48]{2,1,0:T(2,128)(2,1)S(1)}, u32[]{:S(2)}, u32[]{:S(2)}) async-start(bf16[16,1,48]{2,1,0:T(2,128)(2,1)} %convert_element_type.118), calls=%async_computation.5 | async-start | bytes 16384 | tf_op jit(solution)/shard_map/all_to_all | solution.py:99
  317.5 7.4 %fusion.2 = bf16[1,672,3072]{2,1,0:T(8,128)(2,1)} fusion(bf16[768,672]{0,1:T(8,128)(2,1)S(1)} %get-tuple-element.22, bf16[768,3072]{1,0:T(8,128)(2,1)} %bitcast.6), kind=kOutput, calls=%fused_computation.12 | convolution fusion | flops 3172958208 | bytes 9879552 | tf_op jit(solution)/shard_map/sf,sd->fd/dot_general | solution.py:33
  324.9 7.5 %fusion.1 = bf16[1,672,3072]{2,1,0:T(8,128)(2,1)} fusion(bf16[768,672]{0,1:T(8,128)(2,1)S(1)} %get-tuple-element.21, bf16[768,3072]{1,0:T(8,128)(2,1)} %bitcast.3, f32[768]{0:T(1024)S(1)} %reshape.144), kind=kOutput, calls=%fused_computation.11 | convolution fusion | flops 3180036096 | bytes 9882624 | tf_op jit(solution)/shard_map/sf,sd->fd/dot_general | solution.py:39
  332.4 7.3 %fusion.3 = bf16[1,672,3072]{2,1,0:T(8,128)(2,1)} fusion(bf16[768,672]{0,1:T(8,128)(2,1)S(1)} %get-tuple-element.23, bf16[768,3072]{1,0:T(8,128)(2,1)} %bitcast.6), kind=kOutput, calls=%fused_computation.13 | convolution fusion | flops 3172958208 | bytes 9879552 | tf_op jit(solution)/shard_map/sf,sd->fd/dot_general | solution.py:36
  342.2 23.9 %psum.7 = f32[128,4]{1,0:T(8,128)S(1)} all-reduce(f32[128,4]{1,0:T(8,128)S(1)} %reshape.143), channel_id=1, replica_groups=mesh['dp'=8,'expert'=16] {'dp'}, use_global_device_ids=true, to_apply=%region_7.8 | all-reduce | flops 512 | bytes 4096 | tf_op jit(solution)/shard_map/psum | solution.py:112
  (45 shorter events, 13.4 us)
Async XLA Ops:
  7.2 2.8 copy-start
  11.1 26.4 %all-to-all-start = ((bf16[16,1,48]{2,1,0:T(2,128)(2,1)}), bf16[16,1,48]{2,1,0:T(2,128)(2,1)S(1)}, u32[]{:S(2)}, u32[]{:S(2)}) async-start(bf16[16,1,48]{2,1,0:T(2,128)(2,1)} %all_to_all.25), calls=%async_computation | async-start | bytes 16384 | tf_op jit(solution)/shard_map/all_to_all | solution.py:80
  37.5 7.4 %copy-start.3 = (bf16[128,384]{1,0:T(8,128)(2,1)S(1)}, bf16[128,384]{1,0:T(8,128)(2,1)}, u32[]{:S(2)}) copy-start(bf16[128,384]{1,0:T(8,128)(2,1)} %param.8) | copy-start | bytes 294916
  37.5 68.7 %all-to-all-start.2 = ((bf16[16,48,3072]{2,1,0:T(8,128)(2,1)}), bf16[16,48,3072]{2,1,0:T(8,128)(2,1)}, u32[]{:S(2)}, u32[]{:S(2)}) async-start(bf16[16,48,3072]{2,1,0:T(8,128)(2,1)} %bitcast.67), calls=%async_computation.2 | async-start | bytes 9437184 | tf_op jit(solution)/shard_map/all_to_all | solution.py:78
  106.2 77.7 %all-to-all-start.1 = ((bf16[16,48,3072]{2,1,0:T(8,128)(2,1)}), bf16[16,48,3072]{2,1,0:T(8,128)(2,1)}, u32[]{:S(2)}, u32[]{:S(2)}) async-start(bf16[16,48,3072]{2,1,0:T(8,128)(2,1)} %bitcast.66), calls=%async_computation.1 | async-start | bytes 9437184 | tf_op jit(solution)/shard_map/all_to_all | solution.py:79
  124.5 8.4 %copy-start.4 = (bf16[1,672,3072]{2,1,0:T(8,128)(2,1)S(1)}, bf16[1,672,3072]{2,1,0:T(8,128)(2,1)}, u32[]{:S(2)}) copy-start(bf16[1,672,3072]{2,1,0:T(8,128)(2,1)} %param.12) | copy-start | bytes 12386308
  183.9 9.1 %copy-start.2 = (bf16[1,672,3072]{2,1,0:T(8,128)(2,1)S(1)}, bf16[1,672,3072]{2,1,0:T(8,128)(2,1)}, u32[]{:S(2)}) copy-start(bf16[1,672,3072]{2,1,0:T(8,128)(2,1)} %param.11) | copy-start | bytes 12386308
  193.0 4.2 %copy-start.5 = (bf16[1,672,3072]{2,1,0:T(8,128)(2,1)S(1)}, bf16[1,672,3072]{2,1,0:T(8,128)(2,1)}, u32[]{:S(2)}) copy-start(bf16[1,672,3072]{2,1,0:T(8,128)(2,1)} %param.12) | copy-start | bytes 12386308
  203.1 71.8 %all-to-all-start.3 = ((bf16[16,48,3072]{2,1,0:T(8,128)(2,1)}), bf16[16,48,3072]{2,1,0:T(8,128)(2,1)}, u32[]{:S(2)}, u32[]{:S(2)}) async-start(bf16[16,48,3072]{2,1,0:T(8,128)(2,1)} %bitcast.68), calls=%async_computation.3 | async-start | bytes 9437184 | tf_op jit(solution)/shard_map/all_to_all | solution.py:92
  220.0 146.8 %reduce-scatter.2.cloned.1.call-start = ((), (), s32[]{:S(2)}) async-start(), calls=%async_computation.6 | async-start | bytes 1769472 | tf_op jit(solution)/shard_map/reduce_scatter | solution.py:108
  309.1 30.6 %all-to-all-start.4 = ((bf16[16,1,48]{2,1,0:T(2,128)(2,1)}), bf16[16,1,48]{2,1,0:T(2,128)(2,1)S(1)}, u32[]{:S(2)}, u32[]{:S(2)}) async-start(bf16[16,1,48]{2,1,0:T(2,128)(2,1)} %convert_element_type.118), calls=%async_computation.5 | async-start | bytes 16384 | tf_op jit(solution)/shard_map/all_to_all | solution.py:99
  332.4 36.0 %copy-start.1 = (bf16[128,4]{0,1:T(4,128)(2,1)S(1)}, bf16[128,4]{0,1:T(4,128)(2,1)}, u32[]{:S(2)}) copy-start(bf16[128,4]{0,1:T(4,128)(2,1)} %param.10) | copy-start | bytes 3076
Sparse Core Ops, SparseCore 0:
  308.6 34.5 reduce-scatter.1
where the time goes:
time: 376 us; the launch traced here: 375 us
  waiting for transfers between devices  143 us (38%)
  matrix products  64.5 us (17%)
  starting transfers between devices  59.1 us (16%)
  blocking collectives  51.8 us (14%)
  local copies, waits for them, and re-layouts  24.7 us (7%)
  other arithmetic  18.1 us (5%)
  between operations  14.2 us (4%)
    all_to_all x1, waiting for transfers between devices, per_device(): lax.all_to_all(input_part.reshape(experts, capacity, width).astype(jnp.bf...  54.7 us
    all_to_all x1, waiting for transfers between devices, per_device(): lax.all_to_all(send_x, 'expert', split_axis=0, concat_axis=0, tiled=True)  44.2 us
    all_to_all x1, waiting for transfers between devices, per_device(): lax.all_to_all(send_dy, 'expert', split_axis=0, concat_axis=0, tiled=True)  43.8 us
    psum x1, blocking collectives, per_device(): grad_gates = lax.psum(token_gate, 'dp')  23.9 us
    all_to_all x1, starting transfers between devices, per_device(): lax.all_to_all(send_dy, 'expert', split_axis=0, concat_axis=0, tiled=True)  18.2 us
    all_to_all x1, starting transfers between devices, per_device(): lax.all_to_all(input_part.reshape(experts, capacity, width).astype(jnp.bf...  16.9 us
    all_gather x1, blocking collectives, per_device(): lax.all_gather(tokens, 'dp', axis=1, tiled=True)  14.3 us
    all_gather x1, blocking collectives, per_device(): lax.all_gather(grad_out, 'dp', axis=1, tiled=True)  13.6 us
  transfers between devices with their start and end apart: 6, of which 3 were waited for; matrix products, arithmetic and copies ran while one was open for 13% of the time, Pallas kernels for 0%

commit v1 on v0

v1 whole, which is shorter than its diff:
```python
import jax
import jax.numpy as jnp
from jax import lax
from jax.experimental import pallas as pl
from jax.experimental.pallas import tpu as pltpu
from jax.sharding import PartitionSpec as P

MESH = pl.DeviceIdType.MESH
F32, BF16 = jnp.float32, jnp.bfloat16

TOK, D, FS, CAP, NB, TOPK = 128, 3072, 672, 48, 16, 4
DS = D // 8
SLOTS = NB * CAP
CH = 256
NCH = SLOTS // CH

REL = [
    (0, 0), (0, 1), (1, 0), (0, 3), (3, 0), (1, 1),
    (3, 3), (0, 2), (2, 0), (1, 3), (3, 1),
    (1, 2), (2, 1), (3, 2), (2, 3), (2, 2),
]
GROUPS = [(0, 6), (6, 11), (11, 16)]
RETURNS = [(0, 5), (5, 10), (10, 16)]


def split2(v):
    hi = v.astype(BF16)
    lo = (v - hi.astype(F32)).astype(BF16)
    return hi, lo


def nn(a, b):
    return lax.dot_general(a, b, (((1,), (0,)), ((), ())), preferred_element_type=F32)


def nt(a, b):
    return lax.dot_general(a, b, (((1,), (1,)), ((), ())), preferred_element_type=F32)


def tn(a, b):
    return lax.dot_general(a, b, (((0,), (0,)), ((), ())), preferred_element_type=F32)


class Sems:
    def __init__(self, send, recv):
        self.send, self.recv, self.names = send, recv, {}

    def index(self, name):
        return self.names.setdefault(name, len(self.names))


N_SEMS = 140


def main_kernel(
    tok_ref, dy_ref, routes_ref, gates_ref, wg_hbm, wu_hbm, wd_hbm,
    gtok_ref, ggate_ref, xdy_out, hg_out, dg_out, du_out,
    xdy, sel, pick, cols, wg, wu, wd, hg, dg, du, gsend, grecv, grow,
    gpart, gall, gback, ghome, dxf, dxb, sibr, rs_send, rs_recv, rows_back, home,
    send_sems, recv_sems, local_sems,
):
    dp, ex = lax.axis_index("dp"), lax.axis_index("expert")
    y, c = dp // 2, dp % 2
    x, z = ex // 4, ex % 4

    def dev(yy, cc, xx, zz):
        return (lax.rem(yy + 8, 4) * 2 + cc, lax.rem(xx + 8, 4) * 4 + lax.rem(zz + 8, 4))

    up, down, sib = dev(y + 1, c, x, z), dev(y - 1, c, x, z), dev(y, 1 - c, x, z)

    def toward(q):
        return dev(y, c, x - REL[q][0], z - REL[q][1])

    def origin(q):
        return dev(y, c, x + REL[q][0], z + REL[q][1])

    def peer(i):
        return (lax.rem(dp + i, 8), ex)

    sems = Sems(send_sems, recv_sems)
    sent = []

    def copy(name, src, dst, device):
        i = sems.index(name)
        return pltpu.make_async_remote_copy(
            src, dst, sems.send.at[i], sems.recv.at[i], device_id=device, device_id_type=MESH
        )

    def send(name, src, dst, device):
        cp = copy(name, src, dst, device)
        cp.start()
        sent.append(cp)

    def arrive(name, dst, device):
        copy(name, dst, dst, device).wait_recv()

    barrier = pltpu.get_barrier_semaphore()
    partners = [toward(q) for q in range(1, NB)] + [peer(i) for i in range(1, 8)]
    for p in partners:
        pl.semaphore_signal(barrier, inc=1, device_id=p, device_id_type=MESH)

    loads = []
    for i, (src, dst) in enumerate(((wg_hbm, wg), (wu_hbm, wu), (wd_hbm, wd))):
        cp = pltpu.make_async_copy(src.at[0], dst, local_sems.at[i])
        cp.start()
        loads.append(cp)

    r_i = lax.broadcasted_iota(jnp.int32, (TOK, TOK), 0)
    c_i = lax.broadcasted_iota(jnp.int32, (TOK, TOK), 1)
    eye = (r_i == c_i).astype(BF16)
    earlier = (r_i < c_i).astype(BF16)
    rt = tn(routes_ref[...].astype(F32).astype(BF16), eye).astype(jnp.int32)
    gt = tn(gates_ref[...], eye)
    code = ((x + 4 - rt // 4) % 4) * 4 + (z + 4 - rt % 4) % 4
    marks = [(code == a * 4 + b) for a, b in REL]
    count = jnp.concatenate([jnp.sum(m.astype(F32), axis=0, keepdims=True) for m in marks], axis=0)
    gate_of = jnp.concatenate(
        [jnp.sum(jnp.where(m, gt, 0.0), axis=0, keepdims=True) for m in marks], axis=0
    )
    place = nn(count.astype(BF16), earlier)
    place = jnp.where(count > 0, place, -1.0).astype(BF16)
    s_col = lax.broadcasted_iota(jnp.int32, (SLOTS, NB), 0)
    q_col = lax.broadcasted_iota(jnp.int32, (SLOTS, NB), 1)
    spread = ((s_col >= q_col * CAP) & (s_col < q_col * CAP + CAP)).astype(BF16)
    s_row = lax.broadcasted_iota(jnp.int32, (NB, SLOTS), 1)
    q_row = lax.broadcasted_iota(jnp.int32, (NB, SLOTS), 0)
    spread_t = (s_row >= q_row * CAP) & (s_row < q_row * CAP + CAP)
    s_full = lax.broadcasted_iota(jnp.int32, (SLOTS, TOK), 0).astype(F32)
    within = s_full - CAP * jnp.floor((s_full + 0.5) * (1.0 / CAP))
    lane = lax.broadcasted_iota(jnp.int32, (SLOTS, TOK), 1).astype(F32)
    cols[...] = (within == lane).astype(BF16)
    pick[...] = (nn(spread, place) == within).astype(BF16)
    sel[0] = nn(pick[...], tok_ref[...]).astype(BF16)
    sel[1] = nn(pick[...], dy_ref[...]).astype(BF16)
    gate_slots = jnp.where(spread_t, nt(gate_of.astype(BF16), pick[...]), 0.0)
    gate_slots = nn(gate_slots.astype(BF16), cols[...])
    for q in range(NB):
        gsend[q] = jnp.broadcast_to(gate_slots[q : q + 1], (8, TOK))

    pl.semaphore_wait(barrier, len(partners))

    def feat(yy):
        return pl.ds(pl.multiple_of((lax.rem(yy + 8, 4) * 2 + c) * DS, 128), DS)

    def feat_sib(yy):
        return pl.ds(pl.multiple_of((lax.rem(yy + 8, 4) * 2 + 1 - c) * DS, 128), DS)

    def block(q):
        return pl.ds(q * CAP, CAP)

    own0 = pltpu.make_async_copy(sel.at[:, block(0)], xdy.at[:, block(0), feat(y)], local_sems.at[3])
    own0.start()
    for q in range(1, NB):
        send(("x", q), sel.at[:, block(q)], xdy.at[:, block(q), feat(y)], toward(q))
    for q in range(1, NB):
        send(("g", q), gsend.at[q], grecv.at[q], toward(q))
    grecv[0] = gsend[0]

    def halves(g):
        a, b = GROUPS[g][0] * CAP, GROUPS[g][1] * CAP
        mid = a + (b - a + 31) // 32 * 16
        return pl.ds(a, b - a), pl.ds(a, mid - a), pl.ds(mid, b - mid)

    def gather_own(g):
        for q in range(*GROUPS[g]):
            if q == 0:
                own0.wait()
            else:
                arrive(("x", q), xdy.at[:, block(q), feat(y)], origin(q))
        full, _, _ = halves(g)
        mine = xdy.at[:, full, feat(y)]
        send(("up", g), mine, mine, up)
        send(("down", g), mine, mine, down)
        send(("sib", g), mine, mine, sib)

    def gather_relay(g):
        full, first, second = halves(g)
        below = xdy.at[:, full, feat(y - 1)]
        arrive(("up", g), below, down)
        part = xdy.at[:, first, feat(y - 1)]
        send(("up2", g), part, part, up)
        send(("sibb", g), below, below, sib)
        above = xdy.at[:, full, feat(y + 1)]
        arrive(("down", g), above, up)
        part = xdy.at[:, second, feat(y + 1)]
        send(("down2", g), part, part, down)
        send(("siba", g), above, above, sib)

    def gather_end(g):
        full, first, second = halves(g)
        far1, far2 = xdy.at[:, first, feat(y + 2)], xdy.at[:, second, feat(y + 2)]
        arrive(("up2", g), far1, down)
        send(("sib1", g), far1, far1, sib)
        arrive(("down2", g), far2, up)
        send(("sib2", g), far2, far2, sib)
        arrive(("sib", g), xdy.at[:, full, feat_sib(y)], sib)
        arrive(("sibb", g), xdy.at[:, full, feat_sib(y - 1)], sib)
        arrive(("siba", g), xdy.at[:, full, feat_sib(y + 1)], sib)
        arrive(("sib1", g), xdy.at[:, first, feat_sib(y + 2)], sib)
        arrive(("sib2", g), xdy.at[:, second, feat_sib(y + 2)], sib)

    stores = []

    def store(src, dst):
        cp = pltpu.make_async_copy(src, dst, local_sems.at[4 + len(stores)])
        cp.start()
        stores.append(cp)

    half = FS // 2

    def forward(j):
        rows = pl.ds(j * CH, CH)
        lanes = pl.ds(j * CH, CH)

        def step(i, total):
            units = pl.ds(pl.multiple_of(i * half, 16), half)
            pre_gate = nt(wg[units], xdy[0, rows])
            pre_up = nt(wu[units], xdy[0, rows])
            projected = nt(wd[units], xdy[1, rows])
            squash = jax.nn.sigmoid(pre_gate)
            activated = pre_gate * squash
            hidden = (activated * pre_up).astype(BF16).astype(F32)
            total = total + jnp.sum(projected * hidden, axis=0, keepdims=True)
            gates = grow[0:1, lanes]
            hg[units, lanes] = (hidden * gates).astype(BF16)
            grad = gates * projected
            dg[units, lanes] = (
                grad * pre_up * squash * (1.0 + pre_gate * (1.0 - squash))
            ).astype(BF16)
            du[units, lanes] = (grad * activated).astype(BF16)
            return total

        gpart[0:1, lanes] = lax.fori_loop(0, 2, step, jnp.zeros((1, CH), F32))
        store(xdy.at[:, rows], xdy_out.at[:, rows])

    def input_grad(j):
        lanes = pl.ds(j * CH, CH)
        for k in (2, 1, 3, 0):
            yy = lax.rem(y + k, 4)
            feats = pl.ds(pl.multiple_of(yy * 2 * DS, 128), 2 * DS)
            part = tn(dg[:, lanes], wg[:, feats]) + tn(du[:, lanes], wu[:, feats])
            dxf[j, 0, k] = part[:, :DS]
            dxf[j, 1, k] = part[:, DS:]
            dxb[j, k] = dxf[j, 1 - c, k].astype(BF16)
            send(("dx", j, k), dxb.at[j, k], sibr.at[j, k], sib)

    H = CH // 2

    def pair_sum(j, k, rows):
        return dxf[j, c, k, rows] + sibr[j, k, rows].astype(F32)

    lo, hi = pl.ds(0, H), pl.ds(H, H)

    def rs_hop(j, name, slot, value, device):
        rs_send[j, slot] = value.astype(BF16)
        send((name, j), rs_send.at[j, slot], rs_recv.at[j, slot], device)

    def scatter1(j):
        arrive(("dx", j, 2), sibr.at[j, 2], sib)
        rs_hop(j, "f_up", 0, pair_sum(j, 2, lo), up)
        rs_hop(j, "f_down", 1, pair_sum(j, 2, hi), down)
        arrive(("dx", j, 1), sibr.at[j, 1], sib)
        rs_hop(j, "d_up", 2, pair_sum(j, 1, hi), up)
        arrive(("dx", j, 3), sibr.at[j, 3], sib)
        rs_hop(j, "d_down", 3, pair_sum(j, 3, lo), down)

    def scatter2(j):
        arrive(("f_up", j), rs_recv.at[j, 0], down)
        rs_hop(j, "e_up", 4, pair_sum(j, 1, lo) + rs_recv[j, 0].astype(F32), up)
        arrive(("f_down", j), rs_recv.at[j, 1], up)
        rs_hop(j, "e_down", 5, pair_sum(j, 3, hi) + rs_recv[j, 1].astype(F32), down)

    def scatter3(j):
        arrive(("dx", j, 0), sibr.at[j, 0], sib)
        arrive(("d_up", j), rs_recv.at[j, 2], down)
        arrive(("d_down", j), rs_recv.at[j, 3], up)
        arrive(("e_up", j), rs_recv.at[j, 4], down)
        arrive(("e_down", j), rs_recv.at[j, 5], up)
        rows_back[pl.ds(j * CH, H)] = (
            pair_sum(j, 0, lo) + rs_recv[j, 4].astype(F32) + rs_recv[j, 3].astype(F32)
        ).astype(BF16)
        rows_back[pl.ds(j * CH + H, H)] = (
            pair_sum(j, 0, hi) + rs_recv[j, 2].astype(F32) + rs_recv[j, 5].astype(F32)
        ).astype(BF16)
        for q in range(*RETURNS[j]):
            if q > 0:
                send(("r", q), rows_back.at[block(q)], home.at[block(q)], origin(q))

    def gate_rows():
        for q in range(1, NB):
            arrive(("g", q), grecv.at[q], origin(q))
        table = jnp.concatenate([grecv[q, 0:1] for q in range(NB)], axis=0)
        wide = jnp.where(spread_t, nt(table.astype(BF16), cols[...]), 0.0)
        grow[...] = jnp.broadcast_to(jnp.sum(wide, axis=0, keepdims=True), (8, SLOTS))

    def gate_sums():
        wide = jnp.where(spread_t, jnp.broadcast_to(gpart[0:1], (NB, SLOTS)), 0.0)
        h, l = split2(wide)
        gall[dp] = nn(h, cols[...]) + nn(l, cols[...])
        for i in range(1, 8):
            send(("ga", i), gall.at[dp], gall.at[dp], peer(i))

    def gate_back():
        for i in range(1, 8):
            arrive(("ga", i), gall.at[lax.rem(dp + 8 - i, 8)], peer(8 - i))
        total = gall[0]
        for i in range(1, 8):
            total = total + gall[i]
        for q in range(NB):
            gback[q] = jnp.broadcast_to(total[q : q + 1], (8, TOK))
        for q in range(1, NB):
            send(("gr", q), gback.at[q], ghome.at[q], origin(q))
        ghome[0] = gback[0]

    def gate_end():
        for q in range(1, NB):
            arrive(("gr", q), ghome.at[q], toward(q))
        table = jnp.concatenate([ghome[q, 0:1] for q in range(NB)], axis=0)
        h, l = split2(table)
        wide = jnp.where(spread_t, nt(h, cols[...]) + nt(l, cols[...]), 0.0)
        h, l = split2(wide)
        per_token = nn(h, pick[...]) + nn(l, pick[...])
        out = jnp.zeros((TOPK, TOK), F32)
        for q in range(NB):
            out = out + jnp.where(marks[q], jnp.broadcast_to(per_token[q : q + 1], (TOPK, TOK)), 0.0)
        out = jnp.concatenate([out, jnp.zeros((8 - TOPK, TOK), F32)], axis=0)
        ggate_ref[...] = out.T[:, :TOPK]

    gather_own(0)
    gate_rows()
    gather_own(1)
    gather_relay(0)
    gather_own(2)
    for cp in loads:
        cp.wait()
    gather_end(0)
    gather_relay(1)
    forward(0)
    input_grad(0)
    gather_end(1)
    gather_relay(2)
    scatter1(0)
    forward(1)
    scatter2(0)
    input_grad(1)
    gather_end(2)
    scatter1(1)
    scatter3(0)
    forward(2)
    gate_sums()
    scatter2(1)
    input_grad(2)
    scatter1(2)
    scatter3(1)
    store(hg, hg_out)
    store(dg, dg_out)
    store(du, du_out)
    gate_back()
    scatter2(2)
    scatter3(2)
    home[block(0)] = rows_back[block(0)]
    gate_end()
    for q in range(1, NB):
        arrive(("r", q), home.at[block(q)], toward(q))
    gtok_ref[...] = tn(pick[...], home[...]).astype(BF16)
    for cp in sent:
        cp.wait_send()
    for cp in stores:
        cp.wait()


def exchange(tokens, grad_out, routes, gates, w_gate, w_up, w_down):
    vmem = pl.BlockSpec(memory_space=pltpu.VMEM)
    hbm = pl.BlockSpec(memory_space=pl.ANY)
    return pl.pallas_call(
        main_kernel,
        out_shape=(
            jax.ShapeDtypeStruct((TOK, DS), BF16),
            jax.ShapeDtypeStruct((TOK, TOPK), F32),
            jax.ShapeDtypeStruct((2, SLOTS, D), BF16),
            jax.ShapeDtypeStruct((FS, SLOTS), BF16),
            jax.ShapeDtypeStruct((FS, SLOTS), BF16),
            jax.ShapeDtypeStruct((FS, SLOTS), BF16),
        ),
        in_specs=[vmem] * 4 + [hbm] * 3,
        out_specs=(vmem, vmem, hbm, hbm, hbm, hbm),
        scratch_shapes=[
            pltpu.VMEM((2, SLOTS, D), BF16),
            pltpu.VMEM((2, SLOTS, DS), BF16),
            pltpu.VMEM((SLOTS, TOK), BF16),
            pltpu.VMEM((SLOTS, TOK), BF16),
            pltpu.VMEM((FS, D), BF16),
            pltpu.VMEM((FS, D), BF16),
            pltpu.VMEM((FS, D), BF16),
            pltpu.VMEM((FS, SLOTS), BF16),
            pltpu.VMEM((FS, SLOTS), BF16),
            pltpu.VMEM((FS, SLOTS), BF16),
            pltpu.VMEM((NB, 8, TOK), F32),
            pltpu.VMEM((NB, 8, TOK), F32),
            pltpu.VMEM((8, SLOTS), F32),
            pltpu.VMEM((8, SLOTS), F32),
            pltpu.VMEM((8, NB, TOK), F32),
            pltpu.VMEM((NB, 8, TOK), F32),
            pltpu.VMEM((NB, 8, TOK), F32),
            pltpu.VMEM((NCH, 2, 4, CH, DS), F32),
            pltpu.VMEM((NCH, 4, CH, DS), BF16),
            pltpu.VMEM((NCH, 4, CH, DS), BF16),
            pltpu.VMEM((NCH, 6, CH // 2, DS), BF16),
            pltpu.VMEM((NCH, 6, CH // 2, DS), BF16),
            pltpu.VMEM((SLOTS, DS), BF16),
            pltpu.VMEM((SLOTS, DS), BF16),
            pltpu.SemaphoreType.DMA((N_SEMS,)),
            pltpu.SemaphoreType.DMA((N_SEMS,)),
            pltpu.SemaphoreType.DMA((16,)),
        ],
        compiler_params=pltpu.CompilerParams(
            collective_id=0, has_side_effects=True, vmem_limit_bytes=60 << 20
        ),
        cost_estimate=pl.CostEstimate(
            flops=2 * 5 * SLOTS * FS * D, bytes_accessed=25_000_000, transcendentals=SLOTS * FS
        ),
    )(tokens, grad_out, routes, gates, w_gate, w_up, w_down)


def weight_kernel(xdy_ref, hg_ref, dg_ref, du_ref, og_ref, ou_ref, od_ref):
    og_ref[0] = nn(dg_ref[...], xdy_ref[0]).astype(BF16)
    ou_ref[0] = nn(du_ref[...], xdy_ref[0]).astype(BF16)
    od_ref[0] = nn(hg_ref[...], xdy_ref[1]).astype(BF16)


def weight_grads(xdy, hg, dg, du):
    tile = 512
    whole = pl.BlockSpec((FS, SLOTS), lambda i: (0, 0))
    out = pl.BlockSpec((1, FS, tile), lambda i: (0, 0, i))
    shape = jax.ShapeDtypeStruct((1, FS, D), BF16)
    return pl.pallas_call(
        weight_kernel,
        grid=(D // tile,),
        out_shape=(shape, shape, shape),
        in_specs=[pl.BlockSpec((2, SLOTS, tile), lambda i: (0, 0, i)), whole, whole, whole],
        out_specs=(out, out, out),
        compiler_params=pltpu.CompilerParams(vmem_limit_bytes=48 << 20),
        cost_estimate=pl.CostEstimate(
            flops=2 * 3 * SLOTS * FS * D, bytes_accessed=25_000_000, transcendentals=0
        ),
    )(xdy, hg, dg, du)


def per_device(tokens, grad_out, routes, gate_values, w_gate, w_up, w_down):
    grad_tokens, grad_gates, xdy, hg, dg, du = exchange(
        tokens, grad_out, routes, gate_values, w_gate, w_up, w_down
    )
    grad_w_gate, grad_w_up, grad_w_down = weight_grads(xdy, hg, dg, du)
    return grad_tokens, grad_gates, grad_w_gate, grad_w_up, grad_w_down


def solution(mesh):
    return jax.shard_map(
        per_device,
        mesh=mesh,
        in_specs=(
            P("expert", "dp"),
            P("expert", "dp"),
            P("expert", None),
            P("expert", None),
            P("expert", "dp", None),
            P("expert", "dp", None),
            P("expert", "dp", None),
        ),
        out_specs=(
            P("expert", "dp"),
            P("expert", None),
            P("expert", "dp", None),
            P("expert", "dp", None),
            P("expert", "dp", None),
        ),
        check_vma=False,
    )
```

time: 376 us -> 120 us (0.32)
  waiting for transfers between devices: 143 us -> 0 us
  Pallas kernels: 0 us -> 109 us
  matrix products: 64.5 us -> 0 us
  starting transfers between devices: 59.1 us -> 0 us
  blocking collectives: 51.8 us -> 0 us
  other arithmetic: 18.1 us -> 0 us
  local copies, waits for them, and re-layouts: 24.7 us -> 8.61 us
  between operations: 14.2 us -> 0.65 us
    all_to_all x5 -> x0, waiting for transfers between devices: 143 us -> none  [the longest x1 54.7 us: per_device(): lax.all_to_all(input_part.reshape(experts, capacity, width).astype(jnp.bf...]
    pallas_call x0 -> x2, Pallas kernels: none -> 109 us  [the longest x1 96.5 us: exchange(): pl.pallas_call(main_kernel, out_shape=(jax.ShapeDtypeStruct((TOK, DS), BF...]
    dot_general x11 -> x0, matrix products: 64.5 us -> none  [the longest x1 9.12 us: expert_backward(): jnp.einsum('sd,fd->sf', dy_rows, weight_down, preferred_element_type=jnp....]
    all_to_all x5 -> x0, starting transfers between devices: 59.1 us -> none  [the longest x1 18.2 us: per_device(): lax.all_to_all(send_dy, 'expert', split_axis=0, concat_axis=0, tiled=True)]
    all_gather x2 -> x0, blocking collectives: 27.9 us -> none  [the longest x1 14.3 us: per_device(): lax.all_gather(tokens, 'dp', axis=1, tiled=True)]
    psum x1 -> x0, blocking collectives: 23.9 us -> none  [per_device(): grad_gates = lax.psum(token_gate, 'dp')]
    gather x2 -> x0, local copies, waits for them, and re-layouts: 13.2 us -> none  [the longest x1 11 us: combine_rows(): picked = slot_rows[indices]]
    reduce_sum x3 -> x0, other arithmetic: 8.04 us -> none  [the longest x1 7.7 us: combine_rows(): jnp.sum(picked.reshape(tok_rows, top_count, slot_rows.shape[1]), axis=1)]
  transfers between devices with their start and end apart: 6 -> 0, of which waited for: 3 -> 0; matrix products, arithmetic and copies ran while one was open for 13% -> 0% of each run, Pallas kernels for 0% -> 0%
where the time goes in v1:
time: 120 us; the launch traced here: 119 us
  Pallas kernels  109 us (91%)
  local copies, waits for them, and re-layouts  8.61 us (7%)
    pallas_call x1, Pallas kernels, exchange(): pl.pallas_call(main_kernel, out_shape=(jax.ShapeDtypeStruct((TOK, DS), BF...  96.5 us
    pallas_call x1, Pallas kernels, weight_grads(): pl.pallas_call(weight_kernel, grid=(D // tile,), out_shape=(shape, shape,...  13 us
    unnamed x12, local copies, waits for them, and re-layouts  8.61 us

profile of v1, /device:TPU:2, one launch (start us, length us, event | category | flops | bytes accessed | tf_op | source)
XLA Modules:
  0.0 118.7 jit_solution(11783058126136384909)
XLA Ops:
  0.6 1.4 %copy.13.gates_ref = bf16[128,4]{1,0:T(8,128)(2,1)} copy(bf16[128,4]{0,1:T(4,128)(2,1)} %param.10) | data formatting | bytes 2048 | tf_op args[3]
  2.0 1.4 %copy.12.routes_ref = s32[128,4]{1,0:T(8,128)} copy(s32[128,4]{0,1:T(4,128)} %param.9) | data formatting | bytes 4096 | tf_op args[2]
  3.5 96.5 %shard_map.110 = (bf16[128,384]{1,0:T(8,128)(2,1)}, f32[128,4]{1,0:T(8,128)}, bf16[2,768,3072]{2,1,0:T(8,128)(2,1)}, bf16[672,768]{1,0:T(8,128)(2,1)}, bf16[672,...) custom-call(bf16[128,384]{1,0:T(8,128)(2,1)} %tok_ref.1, bf16[128,384]{1,0:T(8,128)(2,1)} %dy_ref.1, s32[128,4]{1,0:T(8,128)} %copy.12.routes_ref, ...), custom_call_target="tpu_custom_call" | custom-call | flops 15854469120 | bytes 25000000 | tf_op jit(solution)/shard_map/pallas_call | solution.py:375
  99.9 1.5 %copy.14 = f32[128,4]{0,1:T(4,128)} copy(f32[128,4]{1,0:T(8,128)} %get-tuple-element.24) | data formatting | bytes 4096
  101.4 0.0 copy-start
  101.4 1.2 %copy-done = bf16[672,768]{1,0:T(8,128)(2,1)S(1)} copy-done((bf16[672,768]{1,0:T(8,128)(2,1)S(1)}, bf16[672,768]{1,0:T(8,128)(2,1)}, u32[]{:S(2)}) %copy-start) | copy-done | bytes 1032216
  102.6 0.0 copy-start.1
  102.6 1.2 %copy-done.1 = bf16[672,768]{1,0:T(8,128)(2,1)S(1)} copy-done((bf16[672,768]{1,0:T(8,128)(2,1)S(1)}, bf16[672,768]{1,0:T(8,128)(2,1)}, u32[]{:S(2)}) %copy-start.1) | copy-done | bytes 1032216
  103.8 0.0 copy-start.2
  103.8 1.2 %copy-done.2 = bf16[672,768]{1,0:T(8,128)(2,1)S(1)} copy-done((bf16[672,768]{1,0:T(8,128)(2,1)S(1)}, bf16[672,768]{1,0:T(8,128)(2,1)}, u32[]{:S(2)}) %copy-start.2) | copy-done | bytes 1032216
  105.1 0.0 copy-start.3
  105.1 13.0 %shard_map.111 = (bf16[1,672,3072]{2,1,0:T(8,128)(2,1)}, bf16[1,672,3072]{2,1,0:T(8,128)(2,1)}, bf16[1,672,3072]{2,1,0:T(8,128)(2,1)}) custom-call(bf16[2,768,3072]{2,1,0:T(8,128)(2,1)} %get-tuple-element.16.xdy_ref, bf16[672,768]{1,0:T(8,128)(2,1)S(1)} %copy-done, bf16[672,768]{1,0:T(8,128)(2,1)S(1)} %copy-done.1, bf16[672,768]{1,0:T(8,128)(2,1)S(1)} %copy-done.2), custom_call_target="tpu_custom_call" | custom-call | flops 9512681472 | bytes 25000000 | tf_op jit(solution)/shard_map/pallas_call | solution.py:436
  118.1 0.0 copy-done.3
  118.1 0.6 copy.16
Async XLA Ops:
  101.4 1.2 %copy-start = (bf16[672,768]{1,0:T(8,128)(2,1)S(1)}, bf16[672,768]{1,0:T(8,128)(2,1)}, u32[]{:S(2)}) copy-start(bf16[672,768]{1,0:T(8,128)(2,1)} %get-tuple-element.17.hg_ref) | copy-start | bytes 3096580
  102.6 1.2 %copy-start.1 = (bf16[672,768]{1,0:T(8,128)(2,1)S(1)}, bf16[672,768]{1,0:T(8,128)(2,1)}, u32[]{:S(2)}) copy-start(bf16[672,768]{1,0:T(8,128)(2,1)} %get-tuple-element.18.dg_ref) | copy-start | bytes 3096580
  103.8 1.2 %copy-start.2 = (bf16[672,768]{1,0:T(8,128)(2,1)S(1)}, bf16[672,768]{1,0:T(8,128)(2,1)}, u32[]{:S(2)}) copy-start(bf16[672,768]{1,0:T(8,128)(2,1)} %get-tuple-element.19.du_ref) | copy-start | bytes 3096580
  105.1 13.0 %copy-start.3 = (bf16[128,384]{1,0:T(8,128)(2,1)S(1)}, bf16[128,384]{1,0:T(8,128)(2,1)}, u32[]{:S(2)}) copy-start(bf16[128,384]{1,0:T(8,128)(2,1)} %get-tuple-element.33) | copy-start | bytes 294916

commit v2 on v1

v2 whole, which is shorter than its diff:
```python
import jax
import jax.numpy as jnp
from jax import lax
from jax.experimental import pallas as pl
from jax.experimental.pallas import tpu as pltpu
from jax.sharding import PartitionSpec as P

MESH = pl.DeviceIdType.MESH
F32, BF16 = jnp.float32, jnp.bfloat16

TOK, D, FS, CAP, NB, TOPK = 128, 3072, 672, 48, 16, 4
DS = D // 8
SLOTS = NB * CAP
CH = 256
NCH = SLOTS // CH

REL = [
    (0, 0), (0, 1), (1, 0), (0, 3), (3, 0), (0, 2), (2, 0),
    (1, 1), (3, 3), (1, 3), (3, 1), (1, 2), (2, 1), (3, 2), (2, 3), (2, 2),
]
OWN = 0
GROUPS = [(7, 11), (11, 16)]
NEAR = (0, 7)
FAR_LIST = [*range(*GROUPS[0]), *range(*GROUPS[1])]
NEAR_LIST = [q for q in range(*NEAR) if q != OWN]
OTHERS = [*range(*GROUPS[0]), *NEAR_LIST, *range(*GROUPS[1])]
N0, NR = NEAR[0] * CAP, (NEAR[1] - NEAR[0]) * CAP
NEAR_ROWS = [(0, 256), (256, NR)]
NEAR_RETURNS = [(0, 5), (5, 7)]
RING_ROWS = [None, ((336, 96), (432, 80)), ((512, 128), (640, 128))]
FAR_RETURNS = [None, (7, 10), (10, 16)]


def split2(v):
    hi = v.astype(BF16)
    lo = (v - hi.astype(F32)).astype(BF16)
    return hi, lo


def nn(a, b):
    return lax.dot_general(a, b, (((1,), (0,)), ((), ())), preferred_element_type=F32)


def nt(a, b):
    return lax.dot_general(a, b, (((1,), (1,)), ((), ())), preferred_element_type=F32)


def tn(a, b):
    return lax.dot_general(a, b, (((0,), (0,)), ((), ())), preferred_element_type=F32)


class Sems:
    def __init__(self, send, recv):
        self.send, self.recv, self.names = send, recv, {}

    def index(self, name):
        return self.names.setdefault(name, len(self.names))


N_SEMS = 208


def main_kernel(
    tok_ref, dy_ref, routes_ref, gates_ref, wg_hbm, wu_hbm, wd_hbm,
    gtok_ref, ggate_ref, x_out, dg_out, du_out, down_out,
    xdy, raw, sel, selb, pick, cols, wg, wu, wd, act, slope, hid, hg, dg, du, stage, gsend, grecv, grow,
    gpart, gall, gback, ghome, dxf, dxb, sibr, rs_send, rs_recv, near_back, near_home,
    tsum, rows_back, home, send_sems, recv_sems, local_sems, load_sems, store_sems, stage_sems,
):
    dp, ex = lax.axis_index("dp"), lax.axis_index("expert")
    y, c = dp // 2, dp % 2
    x, z = ex // 4, ex % 4

    def dev(yy, cc, xx, zz):
        return (lax.rem(yy + 8, 4) * 2 + cc, lax.rem(xx + 8, 4) * 4 + lax.rem(zz + 8, 4))

    up, down, sib = dev(y + 1, c, x, z), dev(y - 1, c, x, z), dev(y, 1 - c, x, z)

    def toward(q):
        return dev(y, c, x - REL[q][0], z - REL[q][1])

    def origin(q):
        return dev(y, c, x + REL[q][0], z + REL[q][1])

    def peer(i):
        return (lax.rem(dp + i, 8), ex)

    sems = Sems(send_sems, recv_sems)
    sent = []

    def copy(name, src, dst, device):
        i = sems.index(name)
        return pltpu.make_async_remote_copy(
            src, dst, sems.send.at[i], sems.recv.at[i], device_id=device, device_id_type=MESH
        )

    def send(name, src, dst, device):
        cp = copy(name, src, dst, device)
        cp.start()
        sent.append(cp)

    def arrive(name, dst, device):
        copy(name, dst, dst, device).wait_recv()

    barrier = pltpu.get_barrier_semaphore()
    partners = [toward(q) for q in OTHERS] + [peer(i) for i in range(1, 8)]
    for p in partners:
        pl.semaphore_signal(barrier, inc=1, device_id=p, device_id_type=MESH)

    def stored(k, cc):
        return pl.ds(pl.multiple_of((lax.rem(y + k, 4) * 2 + cc) * DS, 128), DS)

    loads = []

    def load_weights():
        for i, (src, dst) in enumerate(((wg_hbm, wg), (wu_hbm, wu), (wd_hbm, wd))):
            for k in range(4):
                for cc in range(2):
                    cp = pltpu.make_async_copy(
                        src.at[0, :, stored(k, cc)],
                        dst.at[:, pl.ds((cc * 4 + k) * DS, DS)],
                        load_sems.at[i * 8 + k * 2 + cc],
                    )
                    cp.start()
                    loads.append(cp)

    def feat(k):
        return pl.ds(pl.multiple_of((c * 4 + k) * DS, 128), DS)

    def feat_sib(k):
        return pl.ds(pl.multiple_of(((1 - c) * 4 + k) * DS, 128), DS)

    def block(q):
        return pl.ds(q * CAP, CAP)

    T1, T2 = pl.ds(0, TOK // 2), pl.ds(TOK // 2, TOK // 2)
    raw[0, 0] = tok_ref[...]
    raw[0, 1] = dy_ref[...]

    r_i = lax.broadcasted_iota(jnp.int32, (TOK, TOK), 0)
    c_i = lax.broadcasted_iota(jnp.int32, (TOK, TOK), 1)
    earlier = (r_i < c_i).astype(BF16)
    rt = routes_ref[...]
    gt = gates_ref[...].astype(F32)
    code = ((x + 4 - rt // 4) % 4) * 4 + (z + 4 - rt % 4) % 4
    marks = [(code == a * 4 + b) for a, b in REL]
    count = jnp.concatenate([jnp.sum(m.astype(F32), axis=0, keepdims=True) for m in marks], axis=0)
    gate_of = jnp.concatenate(
        [jnp.sum(jnp.where(m, gt, 0.0), axis=0, keepdims=True) for m in marks], axis=0
    )
    place = nn(count.astype(BF16), earlier)
    place = jnp.where(count > 0, place, -1.0).astype(BF16)
    s_col = lax.broadcasted_iota(jnp.int32, (SLOTS, NB), 0)
    q_col = lax.broadcasted_iota(jnp.int32, (SLOTS, NB), 1)
    spread = ((s_col >= q_col * CAP) & (s_col < q_col * CAP + CAP)).astype(BF16)
    s_row = lax.broadcasted_iota(jnp.int32, (NB, SLOTS), 1)
    q_row = lax.broadcasted_iota(jnp.int32, (NB, SLOTS), 0)
    spread_t = (s_row >= q_row * CAP) & (s_row < q_row * CAP + CAP)
    s_full = lax.broadcasted_iota(jnp.int32, (SLOTS, TOK), 0).astype(F32)
    within = s_full - CAP * jnp.floor((s_full + 0.5) * (1.0 / CAP))
    lane = lax.broadcasted_iota(jnp.int32, (SLOTS, TOK), 1).astype(F32)
    pick[...] = (nn(spread, place) == within).astype(BF16)

    def raw_send(a):
        send(("raw_up", a), raw.at[0, a], raw.at[3, a], up)
        send(("raw_down", a), raw.at[0, a], raw.at[1, a], down)

    def select(a):
        sel[a] = nn(pick[...], raw[0, a]).astype(BF16)

    own = {}

    def own_block(src, a, k):
        cp = pltpu.make_async_copy(src, xdy.at[a, block(OWN), feat(k)], local_sems.at[a * 4 + k])
        cp.start()
        own[a, k] = cp

    def rows_send(a, blocks):
        for q in blocks:
            if q == OWN:
                own_block(sel.at[a, block(OWN)], a, 0)
            else:
                send(("x", q, a), sel.at[a, block(q)], xdy.at[a, block(q), feat(0)], toward(q))

    def gates_send():
        cols[...] = (within == lane).astype(BF16)
        gate_slots = jnp.where(spread_t, nt(gate_of.astype(BF16), pick[...]), 0.0)
        gate_slots = nn(gate_slots.astype(BF16), cols[...])
        for q in range(NB):
            gsend[q] = jnp.broadcast_to(gate_slots[q : q + 1], (8, TOK))
        for q in OTHERS:
            send(("g", q), gsend.at[q], grecv.at[q], toward(q))
        grecv[OWN] = gsend[OWN]

    near = pl.ds(N0, NR)

    def near_send(a, k):
        selb[k - 1, a] = nn(pick[near], raw[k, a]).astype(BF16)
        for q in NEAR_LIST:
            src = selb.at[k - 1, a, pl.ds(q * CAP - N0, CAP)]
            send(("n", q, k, a), src, xdy.at[a, block(q), feat(k)], toward(q))
        own_block(selb.at[k - 1, a, pl.ds(OWN * CAP - N0, CAP)], a, k)

    def raw_relay(a):
        arrive(("raw_up", a), raw.at[3, a], down)
        send(("raw_up2", a), raw.at[3, a, T1], raw.at[2, a, T1], up)
        arrive(("raw_down", a), raw.at[1, a], up)
        send(("raw_down2", a), raw.at[1, a, T2], raw.at[2, a, T2], down)

    def raw_end(a):
        arrive(("raw_up2", a), raw.at[2, a, T1], down)
        arrive(("raw_down2", a), raw.at[2, a, T2], up)

    def near_share(a, k):
        own[a, k].wait()
        for q in NEAR_LIST:
            name = ("x", q, a) if k == 0 else ("n", q, k, a)
            arrive(name, xdy.at[a, block(q), feat(k)], origin(q))
        mine = xdy.at[a, near, feat(k)]
        send(("nsib", k, a), mine, mine, sib)

    def near_end(a):
        for k in range(4):
            arrive(("nsib", k, a), xdy.at[a, near, feat_sib(k)], sib)

    def halves(g):
        a, b = GROUPS[g][0] * CAP, GROUPS[g][1] * CAP
        mid = a + (b - a + 31) // 32 * 16
        return pl.ds(a, b - a), pl.ds(a, mid - a), pl.ds(mid, b - mid)

    def gather_own(g, a):
        for q in range(*GROUPS[g]):
            arrive(("x", q, a), xdy.at[a, block(q), feat(0)], origin(q))
        full, _, _ = halves(g)
        mine = xdy.at[a, full, feat(0)]
        send(("up", g, a), mine, xdy.at[a, full, feat(3)], up)
        send(("down", g, a), mine, xdy.at[a, full, feat(1)], down)
        send(("sib", g, a), mine, mine, sib)

    def gather_relay(g, a):
        full, first, second = halves(g)
        below = xdy.at[a, full, feat(3)]
        arrive(("up", g, a), below, down)
        send(("up2", g, a), xdy.at[a, first, feat(3)], xdy.at[a, first, feat(2)], up)
        above = xdy.at[a, full, feat(1)]
        arrive(("down", g, a), above, up)
        send(("down2", g, a), xdy.at[a, second, feat(1)], xdy.at[a, second, feat(2)], down)
        send(("sibb", g, a), below, below, sib)
        send(("siba", g, a), above, above, sib)

    def gather_end(g, a):
        full, first, second = halves(g)
        far1, far2 = xdy.at[a, first, feat(2)], xdy.at[a, second, feat(2)]
        arrive(("up2", g, a), far1, down)
        send(("sib1", g, a), far1, far1, sib)
        arrive(("down2", g, a), far2, up)
        send(("sib2", g, a), far2, far2, sib)
        arrive(("sib", g, a), xdy.at[a, full, feat_sib(0)], sib)
        arrive(("sibb", g, a), xdy.at[a, full, feat_sib(3)], sib)
        arrive(("siba", g, a), xdy.at[a, full, feat_sib(1)], sib)
        arrive(("sib1", g, a), xdy.at[a, first, feat_sib(2)], sib)
        arrive(("sib2", g, a), xdy.at[a, second, feat_sib(2)], sib)

    stores = []

    def store(src, dst):
        cp = pltpu.make_async_copy(src, dst, store_sems.at[len(stores)])
        cp.start()
        stores.append(cp)

    half = FS // 2

    def gate_up(j):
        rows = pl.ds(j * CH, CH)

        def step(i, carry):
            units = pl.ds(pl.multiple_of(i * half, 16), half)
            pre_gate = nt(wg[units], xdy[0, rows])
            pre_up = nt(wu[units], xdy[0, rows])
            squash = jax.nn.sigmoid(pre_gate)
            activated = pre_gate * squash
            hid[units, rows] = (activated * pre_up).astype(BF16)
            act[j, units] = activated
            slope[j, units] = pre_up * squash * (1.0 + pre_gate * (1.0 - squash))
            return carry

        lax.fori_loop(0, 2, step, 0)
        for k in range(4):
            for cc in range(2):
                src = xdy.at[0, rows, pl.ds((cc * 4 + k) * DS, DS)]
                store(src, x_out.at[rows, stored(k, cc)])

    def hidden_grad(j):
        rows = pl.ds(j * CH, CH)

        def step(i, total):
            units = pl.ds(pl.multiple_of(i * half, 16), half)
            projected = nt(wd[units], xdy[1, rows])
            hidden = hid[units, rows].astype(F32)
            gates = grow[0:1, rows]
            hg[units, rows] = (hidden * gates).astype(BF16)
            grad = gates * projected
            dg[units, rows] = (grad * slope[j, units]).astype(BF16)
            du[units, rows] = (grad * act[j, units]).astype(BF16)
            return total + jnp.sum(projected * hidden, axis=0, keepdims=True)

        gpart[0:1, rows] = lax.fori_loop(0, 2, step, jnp.zeros((1, CH), F32))

    def input_grad(j, ks=(2, 0)):
        rows = pl.ds(j * CH, CH)
        for k in ks:
            for core in (1 - c, c):
                feats = pl.ds(pl.multiple_of((core * 4 + k) * DS, 128), 2 * DS)
                part = tn(dg[:, rows], wg[:, feats]) + tn(du[:, rows], wu[:, feats])
                if core is c:
                    dxf[k, rows] = part[:, :DS]
                    dxf[k + 1, rows] = part[:, DS:]
                else:
                    dxb[k, rows] = part[:, :DS].astype(BF16)
                    dxb[k + 1, rows] = part[:, DS:].astype(BF16)
                    pair = pl.ds(k, 2)
                    send(("dx", j, k), dxb.at[pair, rows], sibr.at[pair, rows], sib)

    def dx_arrive(j, k):
        arrive(("dx", j, k), sibr.at[pl.ds(k, 2), pl.ds(j * CH, CH)], sib)

    def pair_sum(k, rows):
        return dxf[k, rows] + sibr[k, rows].astype(F32)

    pieces = []

    def down_piece(i):
        if i >= 2:
            for cp in pieces[2 * (i - 2) : 2 * (i - 1)]:
                cp.wait()
        cc, k = i // 2, i % 2 * 2
        stage[i % 2] = nn(hg[...], xdy[1, :, pl.ds((cc * 4 + k) * DS, 2 * DS)]).astype(BF16)
        for m in range(2):
            cp = pltpu.make_async_copy(
                stage.at[i % 2, :, pl.ds(m * DS, DS)],
                down_out.at[:, stored(k + m, cc)],
                stage_sems.at[i * 2 + m],
            )
            cp.start()
            pieces.append(cp)

    class RingSum:
        def __init__(self, i, part, first, second):
            self.i, self.part, self.first, self.second = i, part, pl.ds(*first), pl.ds(*second)

        def buffer(self, ref, slot, rows):
            return ref.at[self.i, slot, pl.ds(0, rows.size)]

        def hop(self, name, slot, value, rows, device):
            src = self.buffer(rs_send, slot, rows)
            src[...] = value.astype(BF16)
            send((name, self.i), src, self.buffer(rs_recv, slot, rows), device)

        def take(self, name, slot, rows, device):
            dst = self.buffer(rs_recv, slot, rows)
            arrive((name, self.i), dst, device)
            return dst[...].astype(F32)

        def far(self):
            self.hop("f_up", 0, self.part(2, self.first), self.first, up)
            self.hop("f_down", 1, self.part(2, self.second), self.second, down)
            self.hop("d_down", 3, self.part(3, self.first), self.first, down)

        def near(self):
            self.hop("d_up", 2, self.part(1, self.second), self.second, up)

        def relay(self):
            got = self.take("f_up", 0, self.first, down)
            self.hop("e_up", 4, self.part(1, self.first) + got, self.first, up)
            got = self.take("f_down", 1, self.second, up)
            self.hop("e_down", 5, self.part(3, self.second) + got, self.second, down)

        def sums(self):
            a = self.part(0, self.first) + self.take("d_down", 3, self.first, up)
            a = a + self.take("e_up", 4, self.first, down)
            b = self.part(0, self.second) + self.take("d_up", 2, self.second, down)
            b = b + self.take("e_down", 5, self.second, up)
            return a, b

    rings = [r and RingSum(j, pair_sum, *r) for j, r in enumerate(RING_ROWS)]

    def scatter1(j):
        dx_arrive(j, 2)
        rings[j].far()
        dx_arrive(j, 0)
        rings[j].near()

    def scatter3(j):
        for value, rows in zip(rings[j].sums(), RING_ROWS[j]):
            rows_back[pl.ds(*rows)] = value.astype(BF16)
        for q in range(*FAR_RETURNS[j]):
            send(("r", q), rows_back.at[block(q)], home.at[block(q)], origin(q))

    def near_return(j):
        a, b = NEAR_ROWS[j]
        for k in range(4):
            near_back[k, pl.ds(a - N0, b - a)] = pair_sum(k, pl.ds(a, b - a)).astype(BF16)
        for q in range(*NEAR_RETURNS[j]):
            rows = pl.ds(q * CAP - N0, CAP)
            if q == OWN:
                near_home[:, rows] = near_back[:, rows]
            else:
                send(("nr", q), near_back.at[:, rows], near_home.at[:, rows], origin(q))

    def near_combine():
        for q in NEAR_LIST:
            arrive(("nr", q), near_home.at[:, pl.ds(q * CAP - N0, CAP)], toward(q))
        for k in (2, 1, 3, 0):
            tsum[k] = tn(pick[near], near_home[k])

    token_ring = RingSum(0, lambda k, rows: tsum[k, rows], (0, TOK // 2), (TOK // 2, TOK // 2))

    def gate_rows():
        for q in OTHERS:
            arrive(("g", q), grecv.at[q], origin(q))
        table = jnp.concatenate([grecv[q, 0:1] for q in range(NB)], axis=0)
        wide = jnp.where(spread_t, nt(table.astype(BF16), cols[...]), 0.0)
        grow[...] = jnp.broadcast_to(jnp.sum(wide, axis=0, keepdims=True), (8, SLOTS))

    def gate_sums():
        wide = jnp.where(spread_t, jnp.broadcast_to(gpart[0:1], (NB, SLOTS)), 0.0)
        h, l = split2(wide)
        gall[dp] = nn(h, cols[...]) + nn(l, cols[...])
        for i in range(1, 8):
            send(("ga", i), gall.at[dp], gall.at[dp], peer(i))

    def gate_back():
        for i in range(1, 8):
            arrive(("ga", i), gall.at[lax.rem(dp + 8 - i, 8)], peer(8 - i))
        total = gall[0]
        for i in range(1, 8):
            total = total + gall[i]
        for q in range(NB):
            gback[q] = jnp.broadcast_to(total[q : q + 1], (8, TOK))
        for q in OTHERS:
            send(("gr", q), gback.at[q], ghome.at[q], origin(q))
        ghome[OWN] = gback[OWN]

    def gate_end():
        for q in OTHERS:
            arrive(("gr", q), ghome.at[q], toward(q))
        table = jnp.concatenate([ghome[q, 0:1] for q in range(NB)], axis=0)
        h, l = split2(table)
        wide = jnp.where(spread_t, nt(h, cols[...]) + nt(l, cols[...]), 0.0)
        h, l = split2(wide)
        per_token = nn(h, pick[...]) + nn(l, pick[...])
        out = jnp.zeros((TOPK, TOK), F32)
        for q in range(NB):
            out = out + jnp.where(marks[q], jnp.broadcast_to(per_token[q : q + 1], (TOPK, TOK)), 0.0)
        ggate_ref[...] = out

    far0, far1, close = range(*GROUPS[0]), range(*GROUPS[1]), range(*NEAR)
    select(0)
    pl.semaphore_wait(barrier, len(partners))
    raw_send(0)
    rows_send(0, far0)
    rows_send(0, close)
    raw_send(1)
    rows_send(0, far1)
    select(1)
    load_weights()
    raw_relay(0)
    near_send(0, 3)
    near_send(0, 1)
    gather_own(0, 0)
    raw_relay(1)
    raw_end(0)
    near_send(0, 2)
    rows_send(1, far0)
    rows_send(1, close)
    gather_own(1, 0)
    near_send(1, 3)
    near_send(1, 1)
    gates_send()
    near_share(0, 0)
    rows_send(1, far1)
    raw_end(1)
    near_send(1, 2)
    gather_relay(0, 0)
    near_share(0, 3)
    near_share(0, 1)
    near_share(0, 2)
    near_end(0)
    for cp in loads:
        cp.wait()
    gather_own(0, 1)
    gate_up(0)
    gather_relay(1, 0)
    near_share(1, 0)
    gather_end(0, 0)
    gate_up(1)
    gather_relay(0, 1)
    gather_end(1, 0)
    near_share(1, 3)
    near_share(1, 1)
    gate_up(2)
    gate_rows()
    gather_own(1, 1)
    near_share(1, 2)
    near_end(1)
    hidden_grad(0)
    input_grad(0)
    gather_relay(1, 1)
    gather_end(0, 1)
    hidden_grad(1)
    dx_arrive(0, 2)
    dx_arrive(0, 0)
    near_return(0)
    input_grad(1)
    gather_end(1, 1)
    hidden_grad(2)
    dx_arrive(1, 2)
    rings[1].far()
    dx_arrive(1, 0)
    rings[1].near()
    near_return(1)
    input_grad(2, (2,))
    rings[1].relay()
    input_grad(2, (0,))
    dx_arrive(2, 2)
    rings[2].far()
    dx_arrive(2, 0)
    rings[2].near()
    gate_sums()
    store(dg, dg_out)
    store(du, du_out)
    scatter3(1)
    near_combine()
    down_piece(0)
    rings[2].relay()
    token_ring.far()
    token_ring.near()
    gate_back()
    down_piece(1)
    scatter3(2)
    token_ring.relay()
    down_piece(2)
    gate_end()
    down_piece(3)
    first, second = token_ring.sums()
    for q in FAR_LIST:
        arrive(("r", q), home.at[block(q)], toward(q))
    far_sum = jnp.zeros((TOK, DS), F32)
    for a, b in GROUPS:
        rows = pl.ds(a * CAP, (b - a) * CAP)
        far_sum = far_sum + tn(pick[rows], home[rows])
    gtok_ref[T1] = (far_sum[: TOK // 2] + first).astype(BF16)
    gtok_ref[T2] = (far_sum[TOK // 2 :] + second).astype(BF16)
    for cp in pieces[4:]:
        cp.wait()
    for cp in sent:
        cp.wait_send()
    for cp in stores:
        cp.wait()


def exchange(tokens, grad_out, routes, gates, w_gate, w_up, w_down):
    vmem = pl.BlockSpec(memory_space=pltpu.VMEM)
    hbm = pl.BlockSpec(memory_space=pl.ANY)
    return pl.pallas_call(
        main_kernel,
        out_shape=(
            jax.ShapeDtypeStruct((TOK, DS), BF16),
            jax.ShapeDtypeStruct((TOPK, TOK), F32),
            jax.ShapeDtypeStruct((SLOTS, D), BF16),
            jax.ShapeDtypeStruct((FS, SLOTS), BF16),
            jax.ShapeDtypeStruct((FS, SLOTS), BF16),
            jax.ShapeDtypeStruct((FS, D), BF16),
        ),
        in_specs=[vmem] * 4 + [hbm] * 3,
        out_specs=(vmem, vmem, hbm, hbm, hbm, hbm),
        scratch_shapes=[
            pltpu.VMEM((2, SLOTS, D), BF16),
            pltpu.VMEM((4, 2, TOK, DS), BF16),
            pltpu.VMEM((2, SLOTS, DS), BF16),
            pltpu.VMEM((3, 2, NR, DS), BF16),
            pltpu.VMEM((SLOTS, TOK), BF16),
            pltpu.VMEM((SLOTS, TOK), BF16),
            pltpu.VMEM((FS, D), BF16),
            pltpu.VMEM((FS, D), BF16),
            pltpu.VMEM((FS, D), BF16),
            pltpu.VMEM((NCH, FS, CH), F32),
            pltpu.VMEM((NCH, FS, CH), F32),
            pltpu.VMEM((FS, SLOTS), BF16),
            pltpu.VMEM((FS, SLOTS), BF16),
            pltpu.VMEM((FS, SLOTS), BF16),
            pltpu.VMEM((FS, SLOTS), BF16),
            pltpu.VMEM((2, FS, 2 * DS), BF16),
            pltpu.VMEM((NB, 8, TOK), F32),
            pltpu.VMEM((NB, 8, TOK), F32),
            pltpu.VMEM((8, SLOTS), F32),
            pltpu.VMEM((8, SLOTS), F32),
            pltpu.VMEM((8, NB, TOK), F32),
            pltpu.VMEM((NB, 8, TOK), F32),
            pltpu.VMEM((NB, 8, TOK), F32),
            pltpu.VMEM((4, SLOTS, DS), F32),
            pltpu.VMEM((4, SLOTS, DS), BF16),
            pltpu.VMEM((4, SLOTS, DS), BF16),
            pltpu.VMEM((3, 6, CH // 2, DS), BF16),
            pltpu.VMEM((3, 6, CH // 2, DS), BF16),
            pltpu.VMEM((4, NR, DS), BF16),
            pltpu.VMEM((4, NR, DS), BF16),
            pltpu.VMEM((4, TOK, DS), F32),
            pltpu.VMEM((SLOTS, DS), BF16),
            pltpu.VMEM((SLOTS, DS), BF16),
            pltpu.SemaphoreType.DMA((N_SEMS,)),
            pltpu.SemaphoreType.DMA((N_SEMS,)),
            pltpu.SemaphoreType.DMA((8,)),
            pltpu.SemaphoreType.DMA((24,)),
            pltpu.SemaphoreType.DMA((26,)),
            pltpu.SemaphoreType.DMA((8,)),
        ],
        compiler_params=pltpu.CompilerParams(
            collective_id=0, has_side_effects=True, vmem_limit_bytes=60 << 20
        ),
        cost_estimate=pl.CostEstimate(
            flops=2 * 5 * SLOTS * FS * D, bytes_accessed=25_000_000, transcendentals=SLOTS * FS
        ),
    )(tokens, grad_out, routes.T, gates.T, w_gate, w_up, w_down)


def weight_kernel(
    tok_ref, gate_ref, x_ref, dg_ref, du_ref, down_ref, tok_out, gate_out, og_ref, ou_ref, od_ref
):
    @pl.when(pl.program_id(0) == 0)
    def _():
        tok_out[...] = tok_ref[...]
        gate_out[...] = gate_ref[...]

    og_ref[0] = nn(dg_ref[...], x_ref[...]).astype(BF16)
    ou_ref[0] = nn(du_ref[...], x_ref[...]).astype(BF16)
    od_ref[0] = down_ref[...]


def weight_grads(grad_tokens, grad_gates, x, dg, du, down):
    tile = 512
    whole = pl.BlockSpec((FS, SLOTS), lambda i: (0, 0))
    small = [pl.BlockSpec(a.shape, lambda i: (0, 0)) for a in (grad_tokens, grad_gates)]
    out = pl.BlockSpec((1, FS, tile), lambda i: (0, 0, i))
    shape = jax.ShapeDtypeStruct((1, FS, D), BF16)
    return pl.pallas_call(
        weight_kernel,
        grid=(D // tile,),
        out_shape=(
            jax.ShapeDtypeStruct(grad_tokens.shape, BF16),
            jax.ShapeDtypeStruct(grad_gates.shape, F32),
            shape, shape, shape,
        ),
        in_specs=[
            *small,
            pl.BlockSpec((SLOTS, tile), lambda i: (0, i)),
            whole,
            whole,
            pl.BlockSpec((FS, tile), lambda i: (0, i)),
        ],
        out_specs=(*small, out, out, out),
        compiler_params=pltpu.CompilerParams(vmem_limit_bytes=62 << 20),
        cost_estimate=pl.CostEstimate(
            flops=2 * 2 * SLOTS * FS * D, bytes_accessed=25_000_000, transcendentals=0
        ),
    )(grad_tokens, grad_gates, x, dg, du, down)


def per_device(tokens, grad_out, routes, gate_values, w_gate, w_up, w_down):
    grad_tokens, grad_gates, x, dg, du, down = exchange(
        tokens, grad_out, routes, gate_values, w_gate, w_up, w_down
    )
    grad_tokens, grad_gates, grad_w_gate, grad_w_up, grad_w_down = weight_grads(
        grad_tokens, grad_gates, x, dg, du, down
    )
    return grad_tokens, grad_gates.T, grad_w_gate, grad_w_up, grad_w_down


def solution(mesh):
    return jax.shard_map(
        per_device,
        mesh=mesh,
        in_specs=(
            P("expert", "dp"),
            P("expert", "dp"),
            P("expert", None),
            P("expert", None),
            P("expert", "dp", None),
            P("expert", "dp", None),
            P("expert", "dp", None),
        ),
        out_specs=(
            P("expert", "dp"),
            P("expert", None),
            P("expert", "dp", None),
            P("expert", "dp", None),
            P("expert", "dp", None),
        ),
        check_vma=False,
    )
```

time: 120 us -> 95.9 us (0.80)
  Pallas kernels: 109 us -> 95.1 us
  local copies, waits for them, and re-layouts: 8.61 us -> 0 us
    pallas_call x1, Pallas kernels: 96.5 us -> 82.7 us  [exchange(): pl.pallas_call(main_kernel, out_shape=(jax.ShapeDtypeStruct((TOK, DS), BF...]
    unnamed x12 -> x0, local copies, waits for them, and re-layouts: 8.61 us -> none
where the time goes in v2:
time: 95.9 us; the launch traced here: 95.7 us
  Pallas kernels  95.1 us (99%)
    pallas_call x1, Pallas kernels, exchange(): pl.pallas_call(main_kernel, out_shape=(jax.ShapeDtypeStruct((TOK, DS), BF...  82.7 us
    pallas_call x1, Pallas kernels, weight_grads(): pl.pallas_call(weight_kernel, grid=(D // tile,), out_shape=(jax.ShapeDtyp...  12.3 us

profile of v2, /device:TPU:2, one launch (start us, length us, event | category | flops | bytes accessed | tf_op | source)
XLA Modules:
  0.0 95.7 jit_solution(6161178559147926201)
XLA Ops:
  0.6 82.7 %shard_map.110 = (bf16[128,384]{1,0:T(8,128)(2,1)}, f32[4,128]{1,0:T(4,128)}, bf16[768,3072]{1,0:T(8,128)(2,1)}, bf16[672,768]{1,0:T(8,128)(2,1)}, bf16[672,768]{1,0:T(8,128)(2,1)}, /*index=5*/bf16[672,3072]{1,0:T(8,128)(2,1)}) custom-call(bf16[128,384]{1,0:T(8,128)(2,1)} %tok_ref.1, bf16[128,384]{1,0:T(8,128)(2,1)} %dy_ref.1, s32[4,128]{1,0:T(4,128)} %bitcast.3, ...), custom_call_target="tpu_custom_call" | custom-call | flops 15854469120 | bytes 25000000 | tf_op jit(solution)/shard_map/pallas_call | solution.py:565
  83.4 12.3 %shard_map.111 = (bf16[128,384]{1,0:T(8,128)(2,1)}, f32[4,128]{1,0:T(4,128)}, bf16[1,672,3072]{2,1,0:T(8,128)(2,1)}, bf16[1,672,3072]{2,1,0:T(8,128)(2,1)}, bf16[1,672,3072]{2,1,0:T(8,128)(2,1)}) custom-call(bf16[128,384]{1,0:T(8,128)(2,1)} %get-tuple-element.16.tok_ref, f32[4,128]{1,0:T(4,128)} %get-tuple-element.17.gate_ref, ...), custom_call_target="tpu_custom_call" | custom-call | flops 6341787648 | bytes 25000000 | tf_op jit(solution)/shard_map/pallas_call | solution.py:646

commit v3 on v2

--- a/solution.py
+++ b/solution.py
@@ -98,6 +98,10 @@
         cp = copy(name, src, dst, device)
         cp.start()
         sent.append(cp)
+
+    def drain(rest):
+        while len(sent) > rest:
+            sent.pop(0).wait_send()
 
     def arrive(name, dst, device):
         copy(name, dst, dst, device).wait_recv()
@@ -502,6 +506,7 @@
     gate_rows()
     gather_own(1, 1)
     near_share(1, 2)
+    drain(60)
     near_end(1)
     hidden_grad(0)
     input_grad(0)
@@ -514,6 +519,7 @@
     input_grad(1)
     gather_end(1, 1)
     hidden_grad(2)
+    gate_sums()
     dx_arrive(1, 2)
     rings[1].far()
     dx_arrive(1, 0)
@@ -526,21 +532,21 @@
     rings[2].far()
     dx_arrive(2, 0)
     rings[2].near()
-    gate_sums()
+    gate_back()
     store(dg, dg_out)
     store(du, du_out)
     scatter3(1)
+    rings[2].relay()
     near_combine()
-    down_piece(0)
-    rings[2].relay()
     token_ring.far()
     token_ring.near()
-    gate_back()
-    down_piece(1)
+    down_piece(0)
+    gate_end()
+    drain(50)
     scatter3(2)
     token_ring.relay()
+    down_piece(1)
     down_piece(2)
-    gate_end()
     down_piece(3)
     first, second = token_ring.sums()
     for q in FAR_LIST:
@@ -638,7 +644,7 @@
 
 
 def weight_grads(grad_tokens, grad_gates, x, dg, du, down):
-    tile = 512
+    tile = 768
     whole = pl.BlockSpec((FS, SLOTS), lambda i: (0, 0))
     small = [pl.BlockSpec(a.shape, lambda i: (0, 0)) for a in (grad_tokens, grad_gates)]
     out = pl.BlockSpec((1, FS, tile), lambda i: (0, 0, i))

time: 95.9 us -> 94.5 us (0.985)
  Pallas kernels: 95.1 us -> 93.6 us
where the time goes in v3:
time: 94.5 us; the launch traced here: 94.2 us
  Pallas kernels  93.6 us (99%)
    pallas_call x1, Pallas kernels, exchange(): pl.pallas_call(main_kernel, out_shape=(jax.ShapeDtypeStruct((TOK, DS), BF...  81.9 us
    pallas_call x1, Pallas kernels, weight_grads(): pl.pallas_call(weight_kernel, grid=(D // tile,), out_shape=(jax.ShapeDtyp...  11.6 us

profile of v3, /device:TPU:2, one launch (start us, length us, event | category | flops | bytes accessed | tf_op | source)
XLA Modules:
  0.0 94.2 jit_solution(6373752950165995825)
XLA Ops:
  0.6 81.9 %shard_map.110 = (bf16[128,384]{1,0:T(8,128)(2,1)}, f32[4,128]{1,0:T(4,128)}, bf16[768,3072]{1,0:T(8,128)(2,1)}, bf16[672,768]{1,0:T(8,128)(2,1)}, bf16[672,768]{1,0:T(8,128)(2,1)}, /*index=5*/bf16[672,3072]{1,0:T(8,128)(2,1)}) custom-call(bf16[128,384]{1,0:T(8,128)(2,1)} %tok_ref.1, bf16[128,384]{1,0:T(8,128)(2,1)} %dy_ref.1, s32[4,128]{1,0:T(4,128)} %bitcast.3, ...), custom_call_target="tpu_custom_call" | custom-call | flops 15854469120 | bytes 25000000 | tf_op jit(solution)/shard_map/pallas_call | solution.py:571
  82.6 11.6 %shard_map.111 = (bf16[128,384]{1,0:T(8,128)(2,1)}, f32[4,128]{1,0:T(4,128)}, bf16[1,672,3072]{2,1,0:T(8,128)(2,1)}, bf16[1,672,3072]{2,1,0:T(8,128)(2,1)}, bf16[1,672,3072]{2,1,0:T(8,128)(2,1)}) custom-call(bf16[128,384]{1,0:T(8,128)(2,1)} %get-tuple-element.16.tok_ref, f32[4,128]{1,0:T(4,128)} %get-tuple-element.17.gate_ref, ...), custom_call_target="tpu_custom_call" | custom-call | flops 6341787648 | bytes 25000000 | tf_op jit(solution)/shard_map/pallas_call | solution.py:652

commit v4 on v3

--- a/solution.py
+++ b/solution.py
@@ -509,14 +509,16 @@
     drain(60)
     near_end(1)
     hidden_grad(0)
-    input_grad(0)
+    input_grad(0, (2,))
     gather_relay(1, 1)
+    input_grad(0, (0,))
     gather_end(0, 1)
     hidden_grad(1)
     dx_arrive(0, 2)
     dx_arrive(0, 0)
+    input_grad(1, (2,))
     near_return(0)
-    input_grad(1)
+    input_grad(1, (0,))
     gather_end(1, 1)
     hidden_grad(2)
     gate_sums()

time: 94.5 us -> 96.2 us (1.018)
  Pallas kernels: 93.6 us -> 95.3 us
    pallas_call x1, Pallas kernels: 81.9 us -> 83.6 us  [exchange(): pl.pallas_call(main_kernel, out_shape=(jax.ShapeDtypeStruct((TOK, DS), BF...]
where the time goes in v4:
time: 96.2 us; the launch traced here: 95.9 us
  Pallas kernels  95.3 us (99%)
    pallas_call x1, Pallas kernels, exchange(): pl.pallas_call(main_kernel, out_shape=(jax.ShapeDtypeStruct((TOK, DS), BF...  83.6 us
    pallas_call x1, Pallas kernels, weight_grads(): pl.pallas_call(weight_kernel, grid=(D // tile,), out_shape=(jax.ShapeDtyp...  11.6 us

profile of v4, /device:TPU:2, one launch (start us, length us, event | category | flops | bytes accessed | tf_op | source)
XLA Modules:
  0.0 95.9 jit_solution(15888011084760851154)
XLA Ops:
  0.6 83.6 %shard_map.110 = (bf16[128,384]{1,0:T(8,128)(2,1)}, f32[4,128]{1,0:T(4,128)}, bf16[768,3072]{1,0:T(8,128)(2,1)}, bf16[672,768]{1,0:T(8,128)(2,1)}, bf16[672,768]{1,0:T(8,128)(2,1)}, /*index=5*/bf16[672,3072]{1,0:T(8,128)(2,1)}) custom-call(bf16[128,384]{1,0:T(8,128)(2,1)} %tok_ref.1, bf16[128,384]{1,0:T(8,128)(2,1)} %dy_ref.1, s32[4,128]{1,0:T(4,128)} %bitcast.3, ...), custom_call_target="tpu_custom_call" | custom-call | flops 15854469120 | bytes 25000000 | tf_op jit(solution)/shard_map/pallas_call | solution.py:573
  84.3 11.6 %shard_map.111 = (bf16[128,384]{1,0:T(8,128)(2,1)}, f32[4,128]{1,0:T(4,128)}, bf16[1,672,3072]{2,1,0:T(8,128)(2,1)}, bf16[1,672,3072]{2,1,0:T(8,128)(2,1)}, bf16[1,672,3072]{2,1,0:T(8,128)(2,1)}) custom-call(bf16[128,384]{1,0:T(8,128)(2,1)} %get-tuple-element.16.tok_ref, f32[4,128]{1,0:T(4,128)} %get-tuple-element.17.gate_ref, ...), custom_call_target="tpu_custom_call" | custom-call | flops 6341787648 | bytes 25000000 | tf_op jit(solution)/shard_map/pallas_call | solution.py:654
